TPU v7x, 256 devices: a whole 4x4x8 slice. The times are simulated.
256 devices in a mesh: own: 8 (over z), col: 8 (over x, core), mlp: 4 (over y).
Axes of the slice: x: 4, y: 4, z: 8, core: 2. Of those that a mesh axis runs over, the one named last changes fastest.
Arguments:
- features: bfloat16 [262144, 512], P(('own', 'col')), may hold values from -6 to 6
- nbr_page: int32 [8192, 32], P(('own', 'col')), may hold values from 0 to 262143, as said below
- nbr_weight: bfloat16 [8192, 32], P(('own', 'col')), may hold values from 0.0049743652 to 0.29882812
- labels: int32 [8192], P(('own', 'col')), may hold values from 0 to 255
- w_one: bfloat16 [512, 2048], P(None, 'mlp'), may hold values from -0.25 to 0.25
- w_two: bfloat16 [2048, 256], P('mlp'), may hold values from -0.125 to 0.125
Outputs:
- grad_one: float32 [512, 2048], P(None, 'mlp')
- grad_two: float32 [2048, 256], P('mlp')
Inputs may be any that keep to these rules, and one draw needn't show every extreme that they name: `nbr_page`: page p is held by owner p // 4096 (owners numbered along own then col) at its row p % 4096. The 32 neighbours of a target are distinct pages listed in non-decreasing order of owner. Of the 4096 neighbour entries of the targets of one index of own and col, at most 128 fall on one owner; one owner receives exactly 128 entries from every index, and some owners receive none from some indices.
All inputs are finite; a program needn't handle non-finite values.
Results may differ from a plain program's by a relative error of at most 0.011.
Values may be sent and summed in bfloat16 or wider, within the bound.
No kernel may reach another device: no remote copies, remote signals or barrier semaphores. Data moves between devices by JAX's collectives and lax.ppermute only.
A program may use at most 128 MiB of HBM per device.

v0:
```python
import jax
import jax.numpy as jnp
from jax import lax
from jax.sharding import PartitionSpec as P


def body(features, nbr_page, nbr_weight, labels, w_one, w_two):
    rows_dev = features.shape[0]
    width_f = features.shape[1]
    targets = nbr_page.shape[0]
    width_k = nbr_page.shape[1]
    owners = lax.axis_size(("own", "col"))
    entries = targets * width_k
    capacity = 2 * entries // owners
    owner_ids = nbr_page // rows_dev
    local_row = nbr_page % rows_dev
    owner_range = jnp.arange(owners, dtype=jnp.int32)
    matches = (owner_ids[:, :, None] == owner_range[None, None, :]).astype(jnp.int32)
    row_count = jnp.sum(matches, axis=1)
    earlier_rows = jnp.cumsum(row_count, axis=0) - row_count
    before_owner = jnp.cumsum(row_count, axis=1) - row_count
    first_slot = earlier_rows - before_owner + owner_range[None, :] * capacity
    slot_ids = (
        jnp.sum(matches * first_slot[:, None, :], axis=2)
        + jnp.arange(width_k, dtype=jnp.int32)[None, :]
    )
    flat_slot = slot_ids.reshape(-1)
    requests = jnp.zeros((owners * capacity,), jnp.int32).at[flat_slot].set(local_row.reshape(-1))
    requests = requests.reshape(owners, capacity)
    asked_rows = lax.all_to_all(requests, ("own", "col"), split_axis=0, concat_axis=0, tiled=True)
    fetched = features[asked_rows]
    returned = lax.all_to_all(fetched, ("own", "col"), split_axis=0, concat_axis=0, tiled=True)
    received = returned.reshape(owners * capacity, width_f)
    contract_first = (((0,), (0,)), ((), ()))
    target_ids = jnp.broadcast_to(
        jnp.arange(targets, dtype=jnp.int32)[:, None], (targets, width_k)
    ).reshape(-1)
    spread = (
        jnp.zeros((targets, owners * capacity), jnp.bfloat16)
        .at[target_ids, flat_slot]
        .set(nbr_weight.reshape(-1))
    )
    pre_act = jnp.dot(received, w_one, preferred_element_type=jnp.float32)
    active = jnp.maximum(pre_act, 0.0).astype(jnp.bfloat16)
    hidden = jnp.dot(spread, active, preferred_element_type=jnp.float32).astype(jnp.bfloat16)
    partial_logits = jnp.dot(hidden, w_two, preferred_element_type=jnp.float32)
    logits = lax.psum(partial_logits, "mlp")
    exponent = jnp.exp(logits)
    probability = exponent / jnp.sum(exponent, axis=1, keepdims=True)
    classes = w_two.shape[1]
    onehot_label = (labels[:, None] == jnp.arange(classes, dtype=jnp.int32)[None, :]).astype(
        jnp.float32
    )
    d_logits = (probability - onehot_label).astype(jnp.bfloat16)
    grad_two = lax.dot_general(hidden, d_logits, contract_first, preferred_element_type=jnp.float32)
    d_hidden = lax.dot_general(
        d_logits, w_two, (((1,), (1,)), ((), ())), preferred_element_type=jnp.float32
    ).astype(jnp.bfloat16)
    positive = (pre_act > 0).astype(jnp.float32)
    scattered = lax.dot_general(
        spread, d_hidden, contract_first, preferred_element_type=jnp.float32
    )
    d_pre = (scattered * positive).astype(jnp.bfloat16)
    grad_one = lax.dot_general(received, d_pre, contract_first, preferred_element_type=jnp.float32)
    grad_one, grad_two = lax.psum((grad_one, grad_two), ("own", "col"))
    return (grad_one, grad_two)


def solution(mesh):
    placed = (
        P(("own", "col"), None),
        P(("own", "col"), None),
        P(("own", "col"), None),
        P(("own", "col")),
        P(None, "mlp"),
        P("mlp", None),
    )
    return jax.shard_map(
        body,
        mesh=mesh,
        in_specs=placed,
        out_specs=(P(None, "mlp"), P("mlp", None)),
        check_vma=False,
    )
```

profile of v0, /device:TPU:8, one launch (start us, length us, event | category | flops | bytes accessed | tf_op | source)
XLA Modules:
  0.0 551.1 jit_solution(711926448814235918)
XLA Ops:
  7.2 0.0 copy-start
  7.2 0.8 add_select_fusion
  8.0 0.1 convert_reduce_fusion
  8.1 0.1 copy.16
  8.2 0.1 reduce_window_sum.23
  8.3 0.1 copy.18
  8.4 0.1 copy.22
  8.5 0.1 reshape.163
  8.6 0.2 reduce_window_sum.22
  8.8 0.1 copy.20
  8.8 0.2 select_reduce_fusion
  9.1 0.1 copy.21
  9.2 0.1 add.85
  9.3 0.1 reshape.145
  9.4 15.5 %scatter_custom_fusion = s32[8192]{0:T(1024)S(1)} fusion(s32[4096]{0:T(1024)S(1)} %bitcast.22, s32[4096]{0:T(1024)S(1)} %reshape.163, s32[]{:T(128)} %constant.41.clone.1), kind=kCustom, calls=%fused_computation.34 | custom fusion | bytes 32772 | tf_op jit(solution)/shard_map/scatter | solution.py:28
  25.0 21.3 %all_to_all.17 = s32[64,1,128]{2,1,0:T(1,128)S(1)} all-to-all(s32[64,1,128]{2,1,0:T(1,128)S(1)} %bitcast.23), channel_id=1, replica_groups=mesh['own'=8,'col'=8,'mlp'=4] {'own','col'}, dimensions={0} | all-to-all | bytes 65536 | tf_op jit(solution)/shard_map/all_to_all | solution.py:30
  46.3 36.5 %gather_fusion = bf16[8192,512]{1,0:T(8,128)(2,1)} fusion(bf16[4096,512]{1,0:T(8,128)(2,1)} %param.6, s32[8192]{0:T(1024)S(1)} %fusion.7), kind=kCustom, calls=%fused_computation | custom fusion | bytes 16809984 | tf_op jit(solution)/shard_map/gather | solution.py:31
  82.8 0.0 copy-start.4
  82.8 0.0 copy-start.7
  82.8 0.0 copy-start.6
  82.8 5.9 %all-to-all-start.1 = ((bf16[64,128,512]{2,1,0:T(8,128)(2,1)}), bf16[64,128,512]{2,1,0:T(8,128)(2,1)}, u32[]{:S(2)}, u32[]{:S(2)}) async-start(bf16[64,128,512]{2,1,0:T(8,128)(2,1)} %bitcast.21), calls=%async_computation.1 | async-start | bytes 16777216 | tf_op jit(solution)/shard_map/all_to_all | solution.py:32
  88.7 0.0 all-reduce.4.cloned.1.call-start
  88.8 0.0 copy-done.4
  88.8 0.1 copy.23
  88.9 0.1 reshape.169
  89.0 0.0 copy-done.7
  89.0 0.1 multiply_reduce_fusion
  89.1 0.0 copy-done.6
  89.1 0.1 and_reduce_fusion
  89.3 30.4 %scatter_custom_fusion.1 = bf16[1048576]{0:T(1024)(128)(2,1)} fusion(s32[4096]{0:T(1024)S(1)} %broadcast_select_fusion, bf16[4096]{0:T(1024)(128)(2,1)S(1)} %reshape.169, bf16[]{:T(256)} %constant.50.clone.1), kind=kCustom, calls=%fused_computation.10 | custom fusion | bytes 2097154
  119.7 2.8 reshape.150
  122.5 152.3 %all-to-all-done.1 = bf16[64,128,512]{2,1,0:T(8,128)(2,1)} async-done(((bf16[64,128,512]{2,1,0:T(8,128)(2,1)}), bf16[64,128,512]{2,1,0:T(8,128)(2,1)}, u32[]{:S(2)}, u32[]{:S(2)}) %all-to-all-start.1) | async-done | bytes 8388640 | tf_op jit(solution)/shard_map/all_to_all | solution.py:32
  274.8 0.0 copy-done
  274.8 7.1 %fusion.15 = f32[8192,512]{1,0:T(8,128)S(1)} fusion(bf16[8192,512]{1,0:T(8,128)(2,1)} %bitcast.5, bf16[512,512]{1,0:T(8,128)(2,1)S(1)} %copy-done), kind=kOutput, calls=%fused_computation.43 | convolution fusion | flops 4294967296 | bytes 25690112 | tf_op jit(solution)/shard_map/dot_general | solution.py:43
  281.9 0.0 copy-start.1
  281.9 0.0 copy-start.3
  281.9 0.0 copy-start.5
  281.9 1.6 fusion.3
  283.5 4.1 copy-done.1
  287.6 0.0 copy-done.3
  287.6 0.8 fusion.16
  288.4 0.0 all-reduce.4.cloned.1.call-update
  288.5 0.0 all-reduce.6.cloned.1.call-start
  288.5 42.6 %all-reduce.4.cloned.1.call-done = f32[128,256]{1,0:T(8,128)} async-done(((f32[128,256]{1,0:T(8,128)}), f32[128,256]{1,0:T(8,128)}) %all-reduce.4.cloned.1.call-update) | async-done | bytes 131088 | tf_op jit(solution)/shard_map/psum | solution.py:47
  331.1 1.0 exponential_reduce_fusion
  332.1 0.0 copy-done.5
  332.1 1.1 convolution_convert_fusion
  333.2 0.0 copy-start.2
  333.2 16.1 %fusion.2 = f32[512,512]{1,0:T(8,128)} fusion(bf16[8192,512]{1,0:T(8,128)(2,1)} %bitcast.5, f32[8192,512]{1,0:T(8,128)} %copy-done.1, bf16[128,8192]{1,0:T(8,128)(2,1)S(1)} %reshape.150, bf16[128,512]{1,0:T(8,128)(2,1)S(1)} %convolution_convert_fusion), kind=kOutput, calls=%fused_computation.7 | convolution fusion | flops 5381292032 | bytes 28442624 | tf_op jit(solution)/shard_map/dot_general | solution.py:64
  349.3 0.0 copy-done.2
  349.3 1.1 fusion.14
  350.4 0.0 all-reduce.6.cloned.1.call-update
  350.5 189.7 %all-reduce.6.cloned.1.call-done = (f32[512,512]{1,0:T(8,128)}, f32[512,256]{1,0:T(8,128)}) async-done(((f32[512,512]{1,0:T(8,128)}, f32[512,256]{1,0:T(8,128)}), (f32[512,512]{1,0:T(8,128)}, f32[512,256]{1,0:T(8,128)})) %all-reduce.6.cloned.1.call-update) | async-done | bytes 1572880 | tf_op jit(solution)/shard_map/psum | solution.py:65
  540.2 2.3 copy.27
  542.4 1.9 copy.28
  (7 shorter events, 0.1 us)
Async XLA Ops:
  7.2 267.6 %copy-start = (bf16[512,512]{1,0:T(8,128)(2,1)S(1)}, bf16[512,512]{1,0:T(8,128)(2,1)}, u32[]{:S(2)}) copy-start(bf16[512,512]{1,0:T(8,128)(2,1)} %param.10) | copy-start | bytes 1572868
  82.8 6.0 %copy-start.4 = (bf16[128,32]{0,1:T(8,128)(2,1)S(1)}, bf16[128,32]{0,1:T(8,128)(2,1)}, u32[]{:S(2)}) copy-start(bf16[128,32]{0,1:T(8,128)(2,1)} %param.8) | copy-start | bytes 24580
  82.8 6.2 %copy-start.7 = (s32[2]{0:T(128)S(1)}, s32[2]{0:T(128)}, u32[]{:S(2)}) copy-start(s32[2]{0:T(128)} %constant.51) | copy-start | bytes 28
  82.8 6.3 %copy-start.6 = (s32[2]{0:T(128)S(1)}, s32[2]{0:T(128)}, u32[]{:S(2)}) copy-start(s32[2]{0:T(128)} %constant.54) | copy-start | bytes 28
  82.8 191.9 %all-to-all-start.1 = ((bf16[64,128,512]{2,1,0:T(8,128)(2,1)}), bf16[64,128,512]{2,1,0:T(8,128)(2,1)}, u32[]{:S(2)}, u32[]{:S(2)}) async-start(bf16[64,128,512]{2,1,0:T(8,128)(2,1)} %bitcast.21), calls=%async_computation.1 | async-start | bytes 16777216 | tf_op jit(solution)/shard_map/all_to_all | solution.py:32
  88.7 242.3 %all-reduce.4.cloned.1.call-start = ((), (), s32[]{:S(2)}) async-start(), calls=%async_computation.2 | async-start | bytes 262144 | tf_op jit(solution)/shard_map/psum | solution.py:47
  281.9 5.7 %copy-start.1 = (f32[8192,512]{1,0:T(8,128)}, f32[8192,512]{1,0:T(8,128)S(1)}, u32[]{:S(2)}) copy-start(f32[8192,512]{1,0:T(8,128)S(1)} %fusion.15) | copy-start | bytes 50331652
  281.9 5.7 %copy-start.3 = (bf16[512,256]{1,0:T(8,128)(2,1)S(1)}, bf16[512,256]{1,0:T(8,128)(2,1)}, u32[]{:S(2)}) copy-start(bf16[512,256]{1,0:T(8,128)(2,1)} %param.11) | copy-start | bytes 786436
  281.9 50.2 %copy-start.5 = (s32[128]{0:T(128)S(1)}, s32[128]{0:T(128)}, u32[]{:S(2)}) copy-start(s32[128]{0:T(128)} %param.9) | copy-start | bytes 1540
  288.5 251.7 %all-reduce.6.cloned.1.call-start = ((), (), s32[]{:S(2)}) async-start(), calls=%async_computation.3 | async-start | bytes 3145728 | tf_op jit(solution)/shard_map/psum | solution.py:65
  333.2 16.1 %copy-start.2 = (f32[128,256]{1,0:T(8,128)S(1)}, f32[128,256]{1,0:T(8,128)}, u32[]{:S(2)}) copy-start(f32[128,256]{1,0:T(8,128)} %all-reduce.4.cloned.1.call-done) | copy-start | bytes 393220
Sparse Core Ops, SparseCore 0:
  288.6 42.4 all-reduce.3
  350.6 189.5 all-reduce.5
where the time goes:
time: 552 us; the launch traced here: 551 us
  waiting for transfers between devices  385 us (70%)
  local copies, waits for them, and re-layouts  94.5 us (17%)
  matrix products  27.8 us (5%)
  blocking collectives  21.3 us (4%)
  between operations  14.3 us (3%)
  starting transfers between devices  5.97 us (1%)
    psum x1, waiting for transfers between devices, body(): grad_one, grad_two = lax.psum((grad_one, grad_two), ('own', 'col'))  190 us
    all_to_all x1, waiting for transfers between devices, body(): lax.all_to_all(fetched, ('own', 'col'), split_axis=0, concat_axis=0, tile...  152 us
    psum x1, waiting for transfers between devices, body(): logits = lax.psum(partial_logits, 'mlp')  42.6 us
    unnamed x20, local copies, waits for them, and re-layouts  38.8 us
    gather x1, local copies, waits for them, and re-layouts, body(): fetched = features[asked_rows]  36.5 us
    all_to_all x1, blocking collectives, body(): lax.all_to_all(requests, ('own', 'col'), split_axis=0, concat_axis=0, til...  21.3 us
    dot_general x1, matrix products, body(): lax.dot_general(received, d_pre, contract_first, preferred_element_type=j...  16.1 us
    scatter x1, local copies, waits for them, and re-layouts, body(): jnp.zeros((owners * capacity,), jnp.int32).at[flat_slot]  15.5 us
  transfers between devices with their start and end apart: 3, of which 3 were waited for; matrix products, arithmetic and copies ran while one was open for 6% of the time, Pallas kernels for 0%

commit v1 on v0

--- a/solution.py
+++ b/solution.py
@@ -62,7 +62,7 @@
     )
     d_pre = (scattered * positive).astype(jnp.bfloat16)
     grad_one = lax.dot_general(received, d_pre, contract_first, preferred_element_type=jnp.float32)
-    grad_one, grad_two = lax.psum((grad_one, grad_two), ("own", "col"))
+    grad_one, grad_two = lax.psum(lax.psum((grad_one, grad_two), "own"), "col")
     return (grad_one, grad_two)
 
 

time: 552 us -> 513 us (0.929)
  waiting for transfers between devices: 385 us -> 347 us
    psum x1 -> x2, waiting for transfers between devices: 190 us -> 152 us  [body(): grad_one, grad_two = lax.psum(lax.psum((grad_one, grad_two), 'own'), 'col')]
  transfers between devices with their start and end apart: 3 -> 4, of which waited for: 3 -> 4; matrix products, arithmetic and copies ran while one was open for 6% -> 7% of each run, Pallas kernels for 0% -> 0%
where the time goes in v1:
time: 513 us
  waiting for transfers between devices  347 us (68%)
  local copies, waits for them, and re-layouts  94.5 us (18%)
  matrix products  27.8 us (5%)
  blocking collectives  21.3 us (4%)
  between operations  14 us (3%)
  starting transfers between devices  6.01 us (1%)
    all_to_all x1, waiting for transfers between devices, body(): lax.all_to_all(fetched, ('own', 'col'), split_axis=0, concat_axis=0, tile...  152 us
    psum x2, waiting for transfers between devices, body(): grad_one, grad_two = lax.psum(lax.psum((grad_one, grad_two), 'own'), 'col')  152 us
    psum x1, waiting for transfers between devices, body(): logits = lax.psum(partial_logits, 'mlp')  42.6 us
    unnamed x20, local copies, waits for them, and re-layouts  38.8 us
    gather x1, local copies, waits for them, and re-layouts, body(): fetched = features[asked_rows]  36.5 us
    all_to_all x1, blocking collectives, body(): lax.all_to_all(requests, ('own', 'col'), split_axis=0, concat_axis=0, til...  21.3 us
    dot_general x1, matrix products, body(): lax.dot_general(received, d_pre, contract_first, preferred_element_type=j...  16.1 us
    scatter x1, local copies, waits for them, and re-layouts, body(): jnp.zeros((owners * capacity,), jnp.int32).at[flat_slot]  15.5 us
  transfers between devices with their start and end apart: 4, of which 4 were waited for; matrix products, arithmetic and copies ran while one was open for 7% of the time, Pallas kernels for 0%

profile of v1, /device:TPU:8, one launch (start us, length us, event | category | flops | bytes accessed | tf_op | source)
XLA Modules:
  0.0 512.9 jit_solution(5483480987417255255)
XLA Ops:
  7.2 0.0 copy-start
  7.2 0.8 add_select_fusion
  8.0 0.1 convert_reduce_fusion
  8.1 0.1 copy.16
  8.2 0.1 reduce_window_sum.23
  8.3 0.1 copy.18
  8.4 0.1 copy.22
  8.5 0.1 reshape.163
  8.6 0.2 reduce_window_sum.22
  8.8 0.1 copy.20
  8.8 0.2 select_reduce_fusion
  9.1 0.1 copy.21
  9.2 0.1 add.89
  9.3 0.1 reshape.145
  9.4 15.5 %scatter_custom_fusion = s32[8192]{0:T(1024)S(1)} fusion(s32[4096]{0:T(1024)S(1)} %bitcast.22, s32[4096]{0:T(1024)S(1)} %reshape.163, s32[]{:T(128)} %constant.41.clone.1), kind=kCustom, calls=%fused_computation.34 | custom fusion | bytes 32772 | tf_op jit(solution)/shard_map/scatter | solution.py:28
  25.0 21.3 %all_to_all.17 = s32[64,1,128]{2,1,0:T(1,128)S(1)} all-to-all(s32[64,1,128]{2,1,0:T(1,128)S(1)} %bitcast.23), channel_id=1, replica_groups=mesh['own'=8,'col'=8,'mlp'=4] {'own','col'}, dimensions={0} | all-to-all | bytes 65536 | tf_op jit(solution)/shard_map/all_to_all | solution.py:30
  46.3 36.5 %gather_fusion = bf16[8192,512]{1,0:T(8,128)(2,1)} fusion(bf16[4096,512]{1,0:T(8,128)(2,1)} %param.6, s32[8192]{0:T(1024)S(1)} %fusion.7), kind=kCustom, calls=%fused_computation | custom fusion | bytes 16809984 | tf_op jit(solution)/shard_map/gather | solution.py:31
  82.8 0.0 copy-start.4
  82.8 0.0 copy-start.7
  82.8 0.0 copy-start.6
  82.8 5.9 %all-to-all-start.1 = ((bf16[64,128,512]{2,1,0:T(8,128)(2,1)}), bf16[64,128,512]{2,1,0:T(8,128)(2,1)}, u32[]{:S(2)}, u32[]{:S(2)}) async-start(bf16[64,128,512]{2,1,0:T(8,128)(2,1)} %bitcast.21), calls=%async_computation.1 | async-start | bytes 16777216 | tf_op jit(solution)/shard_map/all_to_all | solution.py:32
  88.7 0.0 all-reduce.6.cloned.1.call-start
  88.8 0.0 copy-done.4
  88.8 0.1 copy.23
  88.9 0.1 reshape.169
  89.0 0.0 copy-done.7
  89.0 0.1 multiply_reduce_fusion
  89.1 0.0 copy-done.6
  89.1 0.1 and_reduce_fusion
  89.3 30.4 %scatter_custom_fusion.1 = bf16[1048576]{0:T(1024)(128)(2,1)} fusion(s32[4096]{0:T(1024)S(1)} %broadcast_select_fusion, bf16[4096]{0:T(1024)(128)(2,1)S(1)} %reshape.169, bf16[]{:T(256)} %constant.50.clone.1), kind=kCustom, calls=%fused_computation.10 | custom fusion | bytes 2097154
  119.7 2.8 reshape.150
  122.5 152.3 %all-to-all-done.1 = bf16[64,128,512]{2,1,0:T(8,128)(2,1)} async-done(((bf16[64,128,512]{2,1,0:T(8,128)(2,1)}), bf16[64,128,512]{2,1,0:T(8,128)(2,1)}, u32[]{:S(2)}, u32[]{:S(2)}) %all-to-all-start.1) | async-done | bytes 8388640 | tf_op jit(solution)/shard_map/all_to_all | solution.py:32
  274.8 0.0 copy-done
  274.8 7.1 %fusion.15 = f32[8192,512]{1,0:T(8,128)S(1)} fusion(bf16[8192,512]{1,0:T(8,128)(2,1)} %bitcast.5, bf16[512,512]{1,0:T(8,128)(2,1)S(1)} %copy-done), kind=kOutput, calls=%fused_computation.43 | convolution fusion | flops 4294967296 | bytes 25690112 | tf_op jit(solution)/shard_map/dot_general | solution.py:43
  281.9 0.0 copy-start.1
  281.9 0.0 copy-start.3
  281.9 0.0 copy-start.5
  281.9 1.6 fusion.3
  283.5 4.1 copy-done.1
  287.6 0.0 copy-done.3
  287.6 0.8 fusion.16
  288.4 0.0 all-reduce.6.cloned.1.call-update
  288.5 0.0 all-reduce.10.cloned.1.call-start
  288.5 42.6 %all-reduce.6.cloned.1.call-done = f32[128,256]{1,0:T(8,128)} async-done(((f32[128,256]{1,0:T(8,128)}), f32[128,256]{1,0:T(8,128)}) %all-reduce.6.cloned.1.call-update) | async-done | bytes 131088 | tf_op jit(solution)/shard_map/psum | solution.py:47
  331.1 1.0 exponential_reduce_fusion
  332.1 0.0 copy-done.5
  332.1 1.1 convolution_convert_fusion
  333.2 0.0 copy-start.2
  333.2 16.1 %fusion.2 = f32[512,512]{1,0:T(8,128)} fusion(bf16[8192,512]{1,0:T(8,128)(2,1)} %bitcast.5, f32[8192,512]{1,0:T(8,128)} %copy-done.1, bf16[128,8192]{1,0:T(8,128)(2,1)S(1)} %reshape.150, bf16[128,512]{1,0:T(8,128)(2,1)S(1)} %convolution_convert_fusion), kind=kOutput, calls=%fused_computation.7 | convolution fusion | flops 5381292032 | bytes 28442624 | tf_op jit(solution)/shard_map/dot_general | solution.py:64
  349.3 0.0 copy-done.2
  349.3 1.1 fusion.14
  350.4 0.0 all-reduce.10.cloned.1.call-update
  350.5 0.0 all-reduce.8.cloned.1.call-start
  350.5 80.5 %all-reduce.10.cloned.1.call-done = (f32[512,512]{1,0:T(8,128)}, f32[512,256]{1,0:T(8,128)}) async-done(((f32[512,512]{1,0:T(8,128)}, f32[512,256]{1,0:T(8,128)}), (f32[512,512]{1,0:T(8,128)}, f32[512,256]{1,0:T(8,128)})) %all-reduce.10.cloned.1.call-update) | async-done | bytes 1572880 | tf_op jit(solution)/shard_map/psum | solution.py:65
  431.0 0.0 all-reduce.8.cloned.1.call-update
  431.0 71.2 %all-reduce.8.cloned.1.call-done = (f32[512,512]{1,0:T(8,128)}, f32[512,256]{1,0:T(8,128)}) async-done(((f32[512,512]{1,0:T(8,128)}, f32[512,256]{1,0:T(8,128)}), (f32[512,512]{1,0:T(8,128)}, f32[512,256]{1,0:T(8,128)})) %all-reduce.8.cloned.1.call-update) | async-done | bytes 1572880 | tf_op jit(solution)/shard_map/psum | solution.py:65
  502.2 2.3 copy.29
  504.5 1.9 copy.30
  (7 shorter events, 0.1 us)
Async XLA Ops:
  7.2 267.6 %copy-start = (bf16[512,512]{1,0:T(8,128)(2,1)S(1)}, bf16[512,512]{1,0:T(8,128)(2,1)}, u32[]{:S(2)}) copy-start(bf16[512,512]{1,0:T(8,128)(2,1)} %param.10) | copy-start | bytes 1572868
  82.8 6.0 %copy-start.4 = (bf16[128,32]{0,1:T(8,128)(2,1)S(1)}, bf16[128,32]{0,1:T(8,128)(2,1)}, u32[]{:S(2)}) copy-start(bf16[128,32]{0,1:T(8,128)(2,1)} %param.8) | copy-start | bytes 24580
  82.8 6.2 %copy-start.7 = (s32[2]{0:T(128)S(1)}, s32[2]{0:T(128)}, u32[]{:S(2)}) copy-start(s32[2]{0:T(128)} %constant.51) | copy-start | bytes 28
  82.8 6.3 %copy-start.6 = (s32[2]{0:T(128)S(1)}, s32[2]{0:T(128)}, u32[]{:S(2)}) copy-start(s32[2]{0:T(128)} %constant.54) | copy-start | bytes 28
  82.8 191.9 %all-to-all-start.1 = ((bf16[64,128,512]{2,1,0:T(8,128)(2,1)}), bf16[64,128,512]{2,1,0:T(8,128)(2,1)}, u32[]{:S(2)}, u32[]{:S(2)}) async-start(bf16[64,128,512]{2,1,0:T(8,128)(2,1)} %bitcast.21), calls=%async_computation.1 | async-start | bytes 16777216 | tf_op jit(solution)/shard_map/all_to_all | solution.py:32
  88.7 242.3 %all-reduce.6.cloned.1.call-start = ((), (), s32[]{:S(2)}) async-start(), calls=%async_computation.2 | async-start | bytes 262144 | tf_op jit(solution)/shard_map/psum | solution.py:47
  281.9 5.7 %copy-start.1 = (f32[8192,512]{1,0:T(8,128)}, f32[8192,512]{1,0:T(8,128)S(1)}, u32[]{:S(2)}) copy-start(f32[8192,512]{1,0:T(8,128)S(1)} %fusion.15) | copy-start | bytes 50331652
  281.9 5.7 %copy-start.3 = (bf16[512,256]{1,0:T(8,128)(2,1)S(1)}, bf16[512,256]{1,0:T(8,128)(2,1)}, u32[]{:S(2)}) copy-start(bf16[512,256]{1,0:T(8,128)(2,1)} %param.11) | copy-start | bytes 786436
  281.9 50.2 %copy-start.5 = (s32[128]{0:T(128)S(1)}, s32[128]{0:T(128)}, u32[]{:S(2)}) copy-start(s32[128]{0:T(128)} %param.9) | copy-start | bytes 1540
  288.5 142.5 %all-reduce.10.cloned.1.call-start = ((), (), s32[]{:S(2)}) async-start(), calls=%async_computation.4 | async-start | bytes 3145728 | tf_op jit(solution)/shard_map/psum | solution.py:65
  333.2 16.1 %copy-start.2 = (f32[128,256]{1,0:T(8,128)S(1)}, f32[128,256]{1,0:T(8,128)}, u32[]{:S(2)}) copy-start(f32[128,256]{1,0:T(8,128)} %all-reduce.6.cloned.1.call-done) | copy-start | bytes 393220
  350.5 151.7 %all-reduce.8.cloned.1.call-start = ((), (), s32[]{:S(2)}) async-start(), calls=%async_computation.3 | async-start | bytes 3145728 | tf_op jit(solution)/shard_map/psum | solution.py:65
Sparse Core Ops, SparseCore 0:
  288.6 42.4 all-reduce.5
  350.6 80.3 all-reduce.9
  433.6 68.5 all-reduce.7
